TPU v7x, 32 devices: a whole 2x2x4 slice. The times are simulated.
32 devices in a mesh: side: 2 (over x), grp: 4 (over z), blk: 4 (over y, core).
Axes of the slice: x: 2, y: 2, z: 4, core: 2. Of those that a mesh axis runs over, the one named last changes fastest.
Arguments:
- embed_codes: bfloat16 [2, 8192, 128], P('side', ('grp', 'blk')), may hold values from -4 to 4
- embed_exps: int32 [2, 64], P('side', ('grp', 'blk')), may hold values from -1 to 1
- degrees: int32 [2, 8192], P('side', ('grp', 'blk')), may hold values from 16 to 128
- adjacency: bfloat16 [2, 1536, 128, 128], P('side', ('grp', 'blk')), may hold values from 0 to 1
- block_index: int32 [2, 2, 1536], P('side', None, ('grp', 'blk')), may hold values from 0 to 16, as said below
Outputs:
- layer_rows: bfloat16 [2, 8192, 128], P('side', ('grp', 'blk'))
Inputs may be any that keep to these rules, and one draw needn't show every extreme that they name: `block_index`: each device's list of 96 slots: its used slots come first, in non-decreasing source tile (row 1 below 16), with distinct (destination, source) pairs and destination tiles below 16; the remaining slots have source 16 and destination 0. Every list uses 96 // 4 slots or more, and in each section one list uses all 96.
All inputs are finite; a program needn't handle non-finite values.
Results may differ from a plain program's by a relative error of at most 0.0048.
Values may be sent and summed in bfloat16 or wider, within the bound.
No kernel may reach another device: no remote copies, remote signals or barrier semaphores. Data moves between devices by JAX's collectives and lax.ppermute only.
A program may use at most 128 MiB of HBM per device.

v0:
```python
import jax
import jax.numpy as jnp
from jax import lax
from jax.sharding import PartitionSpec as P


def swapped(value, axis, stride):
    mask = 2**stride
    pairs = [(source, source ^ mask) for source in range(lax.axis_size(axis))]
    return lax.ppermute(value, axis, pairs)


def scale_rows(codes_part, exps_part, degree_part, tile_rows):
    scale = jnp.repeat(jnp.exp2(exps_part.astype(jnp.float32)), tile_rows, axis=1)
    inverse = lax.rsqrt(degree_part.astype(jnp.float32))
    return (codes_part.astype(jnp.float32) * scale[..., None] * inverse[..., None]).astype(
        jnp.bfloat16
    )


def shards(embed_codes, embed_exps, degrees, adjacency, block_index):
    tile_rows = adjacency.shape[2]
    row_width = embed_codes.shape[2]
    row_count = embed_codes.shape[1]
    tiles_dev = row_count // tile_rows
    groups = lax.axis_size("grp")
    dest_tiles = groups * tiles_dev
    capacity = adjacency.shape[1]
    other_codes, other_exps, other_degrees = swapped((embed_codes, embed_exps, degrees), "side", 0)
    source = scale_rows(other_codes, other_exps, other_degrees, tile_rows)
    panels = source.reshape(tiles_dev, tile_rows, row_width)
    target_tile = block_index[0, 0]
    source_tile = block_index[0, 1]
    own_blocks = adjacency[0]
    starting = jnp.zeros((dest_tiles, tile_rows, row_width), jnp.float32)
    piece = lax.all_gather(panels, "blk", axis=0, tiled=True)
    start = jnp.int32(0)
    piece_tiles = piece.shape[0]
    window = min(piece_tiles * dest_tiles, capacity)
    range_begin = jnp.sum((source_tile < start).astype(jnp.int32))
    range_end = jnp.sum((source_tile < start + piece_tiles).astype(jnp.int32))
    window_start = jnp.minimum(range_begin, capacity - window)
    picked = window_start + jnp.arange(window, dtype=jnp.int32)
    active = (picked >= range_begin) & (picked < range_end)
    offset_tiles = source_tile
    offset_tiles = jnp.clip(offset_tiles, 0, piece_tiles - 1)
    chosen = jnp.take(piece, offset_tiles, axis=0)
    products = jnp.einsum("kij,kjw->kiw", own_blocks, chosen, preferred_element_type=jnp.float32)
    placed = jnp.where(active, target_tile, dest_tiles)
    running = starting.at[placed].add(products, mode="drop")
    summed = lax.psum_scatter(
        running.reshape(groups, row_count, row_width), "grp", scatter_dimension=0, tiled=True
    )
    inverse = lax.rsqrt(degrees.astype(jnp.float32))
    return (summed * inverse[..., None]).astype(jnp.bfloat16)


def solution(mesh):
    placed = (
        P("side", ("grp", "blk"), None),
        P("side", ("grp", "blk")),
        P("side", ("grp", "blk")),
        P("side", ("grp", "blk"), None, None),
        P("side", None, ("grp", "blk")),
    )
    return jax.shard_map(
        shards,
        mesh=mesh,
        in_specs=placed,
        out_specs=P("side", ("grp", "blk"), None),
        check_vma=False,
    )
```

profile of v0, /device:TPU:0, one launch (start us, length us, event | category | flops | bytes accessed | tf_op | source)
XLA Modules:
  0.0 98.5 jit_solution(13596730505723026737)
XLA Ops:
  6.5 0.0 copy-start
  6.5 0.0 reduce-scatter.2.cloned.1.call-start
  6.5 2.9 %collective-permute-start = (bf16[1,512,128]{2,1,0:T(8,128)(2,1)}, bf16[1,512,128]{2,1,0:T(8,128)(2,1)S(1)}, u32[]{:S(2)}, u32[]{:S(2)}) collective-permute-start(bf16[1,512,128]{2,1,0:T(8,128)(2,1)} %param.5), channel_id=1, source_target_pairs={{0,16},{16,0},{1,17},{17,1},{2,18},{18,2},{3,19},{19,3},{4,20},{20... | collective-permute-start | bytes 393224 | tf_op jit(solution)/shard_map/ppermute | solution.py:10
  9.5 0.0 collective-permute-start.2
  9.5 2.0 %collective-permute-start.1 = (s32[1,4]{1,0:T(1,128)}, s32[1,4]{1,0:T(1,128)S(1)}, u32[]{:S(2)}, u32[]{:S(2)}) collective-permute-start(s32[1,4]{1,0:T(1,128)} %param.6), channel_id=1, source_target_pairs={{0,16},{16,0},{1,17},{17,1},{2,18},{18,2},{3,19},{19,3},{4,20},{20... | collective-permute-start | bytes 56 | tf_op jit(solution)/shard_map/ppermute | solution.py:10
  11.5 1.4 %fusion.10 = (s32[]{:T(128)}, s32[]{:T(128)}) fusion(s32[1,2,96]{2,1,0:T(2,128)} %param.9), kind=kLoop, calls=%fused_computation.21 | loop fusion | flops 574 | bytes 392 | tf_op jit(solution)/shard_map/reduce_sum | solution.py:40
  12.9 0.7 compare_and_fusion
  14.2 2.1 %fusion.13 = (s32[96]{0:T(128)S(1)}, s32[96]{0:T(128)S(1)}) fusion(s32[1,2,96]{2,1,0:T(2,128)} %param.9, s32[]{:T(128)} %get-tuple-element.6, s32[]{:T(128)} %get-tuple-element.5, s32[]{:T(128)S(6)} %min.17), kind=kLoop, calls=%fused_computation.24 | loop fusion | flops 1152 | bytes 1548 | tf_op jit(solution)/shard_map/jit(_take)/jit(_where)/select_n | solution.py:47
  16.4 0.0 collective-permute-done.1
  16.4 0.1 broadcast_bitcast_fusion
  16.4 0.0 collective-permute-done.2
  16.5 0.0 collective-permute-done
  16.5 0.2 multiply_convert_fusion.1
  16.7 7.6 %all_gather.3 = bf16[16,128,128]{2,1,0:T(8,128)(2,1)} all-gather(bf16[4,128,128]{2,1,0:T(8,128)(2,1)S(1)} %bitcast.28), channel_id=1, replica_groups=mesh['side'=2,'grp'=4,'blk'=4] {'blk'}, dimensions={0}, use_global_device_ids=true | all-gather | bytes 655360 | tf_op jit(solution)/shard_map/all_gather | solution.py:36
  24.3 3.8 %gather_fusion = bf16[96,128,128]{2,1,0:T(8,128)(2,1)} fusion(bf16[16,128,128]{2,1,0:T(8,128)(2,1)} %all_gather.3, s32[1024]{0:T(1024)S(1)} %pad_clamp_fusion), kind=kCustom, calls=%fused_computation | custom fusion | bytes 6291840 | tf_op jit(solution)/shard_map/jit(_take)/gather | solution.py:47
  28.1 0.0 copy-done
  28.1 7.0 %fusion.4 = f32[96,128,128]{1,2,0:T(8,128)} fusion(bf16[1,96,128,128]{3,2,1,0:T(8,128)(2,1)S(1)} %copy-done, bf16[96,128,128]{2,1,0:T(8,128)(2,1)} %gather_fusion, pred[96]{0:T(512)(128)(4,1)S(1)} %compare_and_fusion), kind=kOutput, calls=%fused_computation.6 | convolution fusion | flops 404226048 | bytes 12583008 | tf_op jit(solution)/shard_map/kij,kjw->kiw/dot_general | solution.py:48
  35.1 6.6 %copy.10 = f32[96,128,128]{2,1,0:T(8,128)} copy(f32[96,128,128]{1,2,0:T(8,128)} %fusion.4) | data formatting | bytes 12582912 | tf_op jit(solution)/shard_map/kij,kjw->kiw/dot_general | solution.py:48
  41.7 1.1 %broadcast_in_dim.23 = f32[16,128,128]{2,1,0:T(8,128)} broadcast(f32[]{:T(128)} %constant.6.clone.1), dimensions={} | broadcast | bytes 1048580 | tf_op jit(solution)/shard_map/broadcast_in_dim | solution.py:35
  42.8 18.7 %scatter_fusion = f32[16,128,128]{2,1,0:T(8,128)} fusion(f32[16,128,128]{2,1,0:T(8,128)} %broadcast_in_dim.23, s32[96]{0:T(128)S(1)} %get-tuple-element.8, f32[96,128,128]{2,1,0:T(8,128)} %copy.10), kind=kCustom, calls=%fused_computation.1 | custom fusion | flops 1572864 | bytes 18874752 | tf_op jit(solution)/shard_map/scatter-add | solution.py:50
  61.5 0.0 reduce-scatter.2.cloned.1.call-update
  61.5 0.0 copy-done.1
  61.5 28.4 %reduce-scatter.2.cloned.1.call-done = f32[1,512,128]{2,1,0:T(8,128)} async-done(((f32[4,512,128]{2,1,0:T(8,128)}), f32[1,512,128]{2,1,0:T(8,128)}) %reduce-scatter.2.cloned.1.call-update) | async-done | bytes 262160 | tf_op jit(solution)/shard_map/reduce_scatter | solution.py:51
  90.0 1.7 %multiply_convert_fusion = bf16[1,512,128]{2,1,0:T(8,128)(2,1)} fusion(f32[1,512,128]{2,1,0:T(8,128)} %reduce-scatter.2.cloned.1.call-done, f32[512]{0:T(512)S(1)} %bitcast.30), kind=kLoop, calls=%fused_computation.8 | loop fusion | flops 131072 | bytes 395264 | tf_op jit(solution)/shard_map/convert_element_type | solution.py:55
  (5 shorter events, 0.0 us)
Async XLA Ops:
  6.5 21.6 %copy-start = (bf16[1,96,128,128]{3,2,1,0:T(8,128)(2,1)S(1)}, bf16[1,96,128,128]{3,2,1,0:T(8,128)(2,1)}, u32[]{:S(2)}) copy-start(bf16[1,96,128,128]{3,2,1,0:T(8,128)(2,1)} %param.8) | copy-start | bytes 9437188
  6.5 83.4 %reduce-scatter.2.cloned.1.call-start = ((), (), s32[]{:S(2)}) async-start(), calls=%async_computation.1 | async-start | bytes 1310720 | tf_op jit(solution)/shard_map/reduce_scatter | solution.py:51
  6.5 9.9 %collective-permute-start = (bf16[1,512,128]{2,1,0:T(8,128)(2,1)}, bf16[1,512,128]{2,1,0:T(8,128)(2,1)S(1)}, u32[]{:S(2)}, u32[]{:S(2)}) collective-permute-start(bf16[1,512,128]{2,1,0:T(8,128)(2,1)} %param.5), channel_id=1, source_target_pairs={{0,16},{16,0},{1,17},{17,1},{2,18},{18,2},{3,19},{19,3},{4,20},{20... | collective-permute-start | bytes 393224 | tf_op jit(solution)/shard_map/ppermute | solution.py:10
  9.5 7.0 %collective-permute-start.2 = (s32[1,512]{1,0:T(1,128)}, s32[1,512]{1,0:T(1,128)S(1)}, u32[]{:S(2)}, u32[]{:S(2)}) collective-permute-start(s32[1,512]{1,0:T(1,128)} %param.7), channel_id=1, source_target_pairs={{0,16},{16,0},{1,17},{17,1},{2,18},{18,2},{3,19},{19,3},{4,20},{20... | collective-permute-start | bytes 6152 | tf_op jit(solution)/shard_map/ppermute | solution.py:10
  9.5 6.8 %collective-permute-start.1 = (s32[1,4]{1,0:T(1,128)}, s32[1,4]{1,0:T(1,128)S(1)}, u32[]{:S(2)}, u32[]{:S(2)}) collective-permute-start(s32[1,4]{1,0:T(1,128)} %param.6), channel_id=1, source_target_pairs={{0,16},{16,0},{1,17},{17,1},{2,18},{18,2},{3,19},{19,3},{4,20},{20... | collective-permute-start | bytes 56 | tf_op jit(solution)/shard_map/ppermute | solution.py:10
  42.8 18.7 %copy-start.1 = (s32[1,512]{1,0:T(1,128)S(1)}, s32[1,512]{1,0:T(1,128)}, u32[]{:S(2)}) copy-start(s32[1,512]{1,0:T(1,128)} %param.7) | copy-start | bytes 6148
Sparse Core Ops, SparseCore 0:
  61.6 28.2 reduce-scatter.1
where the time goes:
time: 98.9 us; the launch traced here: 98.5 us
  waiting for transfers between devices  28.4 us (29%)
  other arithmetic  24.8 us (25%)
  between operations  14.1 us (14%)
  local copies, waits for them, and re-layouts  11.6 us (12%)
  blocking collectives  7.65 us (8%)
  matrix products  7.01 us (7%)
  starting transfers between devices  4.97 us (5%)
    reduce_scatter x1, waiting for transfers between devices, shards(): lax.psum_scatter(running.reshape(groups, row_count, row_width), 'grp', sc...  28.4 us
    scatter-add x1, other arithmetic, shards(): running = starting.at[placed].add(products, mode='drop')  18.7 us
    all_gather x1, blocking collectives, shards(): piece = lax.all_gather(panels, 'blk', axis=0, tiled=True)  7.65 us
    dot_general x1, matrix products, shards(): jnp.einsum('kij,kjw->kiw', own_blocks, chosen, preferred_element_type=jnp...  7.01 us
    dot_general x1, local copies, waits for them, and re-layouts, shards(): jnp.einsum('kij,kjw->kiw', own_blocks, chosen, preferred_element_type=jnp...  6.6 us
    ppermute x3, starting transfers between devices, swapped(): return lax.ppermute(value, axis, pairs)  4.96 us
    gather x1, local copies, waits for them, and re-layouts, shards(): chosen = jnp.take(piece, offset_tiles, axis=0)  3.76 us
    select_n x1, other arithmetic, shards(): chosen = jnp.take(piece, offset_tiles, axis=0)  2.1 us
  transfers between devices with their start and end apart: 4, of which 1 were waited for; matrix products, arithmetic and copies ran while one was open for 4% of the time, Pallas kernels for 0%

commit v1 on v0

v1 whole, which is shorter than its diff:
```python
import functools

import jax
import jax.numpy as jnp
from jax import lax
from jax.experimental import pallas as pl
from jax.experimental.pallas import tpu as pltpu
from jax.sharding import PartitionSpec as P


def scale_rows(codes_part, exps_part, degree_part, tile_rows):
    scale = jnp.repeat(jnp.exp2(exps_part.astype(jnp.float32)), tile_rows, axis=1)
    inverse = lax.rsqrt(degree_part.astype(jnp.float32))
    return (codes_part.astype(jnp.float32) * scale[..., None] * inverse[..., None]).astype(
        jnp.bfloat16
    )


def block_kernel(blks, groups, tiles_dev, unroll, index_ref, place_ref, *refs):
    panels = refs[:blks]
    blocks = refs[blks]
    outs = refs[blks + 1 : blks + 1 + groups]
    source, total = refs[blks + 1 + groups :]
    my_blk = place_ref[0]
    my_grp = place_ref[1]
    source_tiles = blks * tiles_dev
    dest_tiles = groups * tiles_dev
    capacity = blocks.shape[0]
    for hop in range(blks):
        source[pl.ds((my_blk ^ hop) * tiles_dev, tiles_dev)] = panels[hop][...]
    total[...] = jnp.zeros_like(total)

    def step(slot):
        target = index_ref[0, slot]
        origin = index_ref[1, slot]
        held = origin < source_tiles
        target = jnp.where(held, target, dest_tiles)
        origin = jnp.where(held, origin, 0)
        return target, jnp.dot(
            blocks[slot], source[origin], preferred_element_type=jnp.float32
        )

    @pl.loop(0, capacity // unroll)
    def _(batch):
        made = [step(batch * unroll + part) for part in range(unroll)]
        for target, product in made:
            total[target] += product

    for hop in range(groups):
        mine = total[pl.ds((my_grp ^ hop) * tiles_dev, tiles_dev)]
        outs[hop][...] = mine.astype(outs[hop].dtype)


def propagate(index, place, panels, blocks, groups):
    blks = len(panels)
    tiles_dev, tile_rows, row_width = panels[0].shape
    capacity = blocks.shape[0]
    unroll = next(size for size in (8, 4, 2, 1) if capacity % size == 0)
    vmem = pl.BlockSpec(memory_space=pltpu.VMEM)
    smem = pl.BlockSpec(memory_space=pltpu.SMEM)
    part = (tiles_dev, tile_rows, row_width)
    return pl.pallas_call(
        functools.partial(block_kernel, blks, groups, tiles_dev, unroll),
        out_shape=[
            jax.ShapeDtypeStruct(part, jnp.float32 if hop == 0 else jnp.bfloat16)
            for hop in range(groups)
        ],
        in_specs=[smem, smem] + [vmem] * (blks + 1),
        out_specs=[vmem] * groups,
        scratch_shapes=[
            pltpu.VMEM((blks * tiles_dev, tile_rows, row_width), jnp.bfloat16),
            pltpu.VMEM((groups * tiles_dev + 1, tile_rows, row_width), jnp.float32),
        ],
        compiler_params=pltpu.CompilerParams(vmem_limit_bytes=48 * 1024 * 1024),
        cost_estimate=pl.CostEstimate(
            flops=2 * capacity * tile_rows * tile_rows * row_width,
            bytes_accessed=2 * capacity * tile_rows * tile_rows,
            transcendentals=0,
        ),
    )(index, place, *panels, blocks)


def shards(embed_codes, embed_exps, degrees, adjacency, block_index):
    tile_rows = adjacency.shape[2]
    row_width = embed_codes.shape[2]
    row_count = embed_codes.shape[1]
    tiles_dev = row_count // tile_rows
    groups = lax.axis_size("grp")
    blks = lax.axis_size("blk")
    source = scale_rows(embed_codes, embed_exps, degrees, tile_rows)
    panel = lax.ppermute(
        source.reshape(tiles_dev, tile_rows, row_width), "side", [(0, 1), (1, 0)]
    )
    panels = [panel] + [
        lax.ppermute(panel, "blk", [(at, at ^ hop) for at in range(blks)])
        for hop in range(1, blks)
    ]
    place = jnp.stack([lax.axis_index("blk"), lax.axis_index("grp")]).astype(jnp.int32)
    parts = propagate(block_index[0], place, panels, adjacency[0], groups)
    summed = parts[0]
    for hop in range(1, groups):
        arrived = lax.ppermute(parts[hop], "grp", [(at, at ^ hop) for at in range(groups)])
        summed = summed + arrived.astype(jnp.float32)
    inverse = lax.rsqrt(degrees.astype(jnp.float32))
    return (summed.reshape(1, row_count, row_width) * inverse[..., None]).astype(jnp.bfloat16)


def solution(mesh):
    placed = (
        P("side", ("grp", "blk"), None),
        P("side", ("grp", "blk")),
        P("side", ("grp", "blk")),
        P("side", ("grp", "blk"), None, None),
        P("side", None, ("grp", "blk")),
    )
    return jax.shard_map(
        shards,
        mesh=mesh,
        in_specs=placed,
        out_specs=P("side", ("grp", "blk"), None),
        check_vma=False,
    )
```

time: 98.9 us -> 39.6 us (0.40)
  other arithmetic: 24.8 us -> 3.38 us
  between operations: 14.1 us -> 0.03 us
  local copies, waits for them, and re-layouts: 11.6 us -> 2.64 us
  waiting for transfers between devices: 28.4 us -> 20.5 us
  blocking collectives: 7.65 us -> 0 us
  matrix products: 7.01 us -> 0 us
  starting transfers between devices: 4.97 us -> 9.38 us
  Pallas kernels: 0 us -> 3.54 us
    reduce_scatter x1 -> x0, waiting for transfers between devices: 28.4 us -> none  [shards(): lax.psum_scatter(running.reshape(groups, row_count, row_width), 'grp', sc...]
    ppermute x3 -> x7, waiting for transfers between devices: 0.01 us -> 20.5 us  [the longest x3 10.3 us: shards(): lax.ppermute(parts[hop], 'grp', [(at, at ^ hop) for at in range(groups)])]
    scatter-add x1 -> x0, other arithmetic: 18.7 us -> none  [shards(): running = starting.at[placed].add(products, mode='drop')]
    all_gather x1 -> x0, blocking collectives: 7.65 us -> none  [shards(): piece = lax.all_gather(panels, 'blk', axis=0, tiled=True)]
    dot_general x1 -> x0, matrix products: 7.01 us -> none  [shards(): jnp.einsum('kij,kjw->kiw', own_blocks, chosen, preferred_element_type=jnp...]
    dot_general x1 -> x0, local copies, waits for them, and re-layouts: 6.6 us -> none  [shards(): jnp.einsum('kij,kjw->kiw', own_blocks, chosen, preferred_element_type=jnp...]
    ppermute x3 -> x7, starting transfers between devices: 4.96 us -> 9.38 us  [the longest x3 4.48 us: shards(): lax.ppermute(parts[hop], 'grp', [(at, at ^ hop) for at in range(groups)])]
    gather x1 -> x0, local copies, waits for them, and re-layouts: 3.76 us -> none  [shards(): chosen = jnp.take(piece, offset_tiles, axis=0)]
  transfers between devices with their start and end apart: 4 -> 7, of which waited for: 1 -> 5; matrix products, arithmetic and copies ran while one was open for 4% -> 0% of each run, Pallas kernels for 0% -> 0%
where the time goes in v1:
time: 39.6 us; the launch traced here: 39.4 us
  waiting for transfers between devices  20.5 us (52%)
  starting transfers between devices  9.38 us (24%)
  Pallas kernels  3.54 us (9%)
  other arithmetic  3.38 us (9%)
  local copies, waits for them, and re-layouts  2.64 us (7%)
    ppermute x3, waiting for transfers between devices, shards(): lax.ppermute(parts[hop], 'grp', [(at, at ^ hop) for at in range(groups)])  10.3 us
    ppermute x3, waiting for transfers between devices, shards(): lax.ppermute(panel, 'blk', [(at, at ^ hop) for at in range(blks)])  6.63 us
    ppermute x3, starting transfers between devices, shards(): lax.ppermute(parts[hop], 'grp', [(at, at ^ hop) for at in range(groups)])  4.48 us
    pallas_call x1, Pallas kernels, propagate(): pl.pallas_call(functools.partial(block_kernel, blks, groups, tiles_dev, u...  3.54 us
    ppermute x1, waiting for transfers between devices, shards(): lax.ppermute(source.reshape(tiles_dev, tile_rows, row_width), 'side', [(0...  3.5 us
    ppermute x1, starting transfers between devices, shards(): lax.ppermute(source.reshape(tiles_dev, tile_rows, row_width), 'side', [(0...  3 us
    unnamed x4, local copies, waits for them, and re-layouts  2.57 us
    ppermute x3, starting transfers between devices, shards(): lax.ppermute(panel, 'blk', [(at, at ^ hop) for at in range(blks)])  1.9 us
  transfers between devices with their start and end apart: 7, of which 5 were waited for; matrix products, arithmetic and copies ran while one was open for 0% of the time, Pallas kernels for 0%

profile of v1, /device:TPU:0, one launch (start us, length us, event | category | flops | bytes accessed | tf_op | source)
XLA Modules:
  0.0 39.4 jit_solution(15146076159105886032)
XLA Ops:
  0.0 0.7 %exponential_bitcast_fusion = f32[4]{0:T(128)S(1)} fusion(s32[1,4]{1,0:T(1,128)} %param.6), kind=kLoop, calls=%fused_computation.7 | loop fusion | flops 8 | bytes 32 | tf_op jit(solution)/shard_map/exp2 | solution.py:12
  0.7 0.1 broadcast_bitcast_fusion
  0.7 0.7 %convert_rsqrt_fusion = f32[1,512]{1,0:T(1,128)S(1)} fusion(s32[1,512]{1,0:T(1,128)} %param.7), kind=kLoop, calls=%fused_computation.4 | loop fusion | flops 512 | bytes 4096 | tf_op jit(solution)/shard_map/rsqrt | solution.py:13
  1.4 1.1 %multiply_convert_fusion = bf16[1,512,128]{2,1,0:T(8,128)(2,1)S(1)} fusion(bf16[1,512,128]{2,1,0:T(8,128)(2,1)} %param.5, f32[512]{0:T(512)S(1)} %bitcast.19, f32[512]{0:T(512)S(1)} %broadcast_bitcast_fusion), kind=kLoop, calls=%fused_computation.3 | loop fusion | flops 262144 | bytes 266240 | tf_op jit(solution)/shard_map/convert_element_type | solution.py:14
  2.5 3.0 %collective-permute-start = (bf16[4,128,128]{2,1,0:T(8,128)(2,1)S(1)}, bf16[4,128,128]{2,1,0:T(8,128)(2,1)S(1)}, u32[]{:S(2)}, u32[]{:S(2)}) collective-permute-start(bf16[4,128,128]{2,1,0:T(8,128)(2,1)S(1)} %bitcast.18), channel_id=1, source_target_pairs={{0,16},{16,0},{1,17},{17,1},{2,18},{18,2},{3,19},{19,3},{4,20},{20... | collective-permute-start | bytes 393224 | tf_op jit(solution)/shard_map/ppermute | solution.py:91
  5.5 3.5 %collective-permute-done.refs_0_ = bf16[4,128,128]{2,1,0:T(8,128)(2,1)S(1)} collective-permute-done((bf16[4,128,128]{2,1,0:T(8,128)(2,1)S(1)}, bf16[4,128,128]{2,1,0:T(8,128)(2,1)S(1)}, u32[]{:S(2)}, u32[]{:S(2)}) %collective-permute-start) | collective-permute-done | bytes 131104 | tf_op jit(solution)/shard_map/ppermute | solution.py:91
  9.0 0.3 collective-permute-start.3
  9.4 1.5 %collective-permute-start.2 = (bf16[4,128,128]{2,1,0:T(8,128)(2,1)S(1)}, bf16[4,128,128]{2,1,0:T(8,128)(2,1)S(1)}, u32[]{:S(2)}, u32[]{:S(2)}) collective-permute-start(bf16[4,128,128]{2,1,0:T(8,128)(2,1)S(1)} %collective-permute-done.refs_0_), channel_id=1, source_target_pairs={{0,2},{1,3},{2,0},{3,1},{4,6},{5,7},{6,4},{7,5},{8,10},{9,11},{10,... | collective-permute-start | bytes 393224 | tf_op jit(solution)/shard_map/ppermute | solution.py:95
  10.8 0.1 collective-permute-start.1
  10.9 0.1 pad_add_fusion.place_ref
  11.0 3.5 %collective-permute-done.3.refs_3_ = bf16[4,128,128]{2,1,0:T(8,128)(2,1)S(1)} collective-permute-done((bf16[4,128,128]{2,1,0:T(8,128)(2,1)S(1)}, bf16[4,128,128]{2,1,0:T(8,128)(2,1)S(1)}, u32[]{:S(2)}, u32[]{:S(2)}) %collective-permute-start.3) | collective-permute-done | bytes 131104 | tf_op jit(solution)/shard_map/ppermute | solution.py:95
  14.5 3.1 %collective-permute-done.2.refs_2_ = bf16[4,128,128]{2,1,0:T(8,128)(2,1)S(1)} collective-permute-done((bf16[4,128,128]{2,1,0:T(8,128)(2,1)S(1)}, bf16[4,128,128]{2,1,0:T(8,128)(2,1)S(1)}, u32[]{:S(2)}, u32[]{:S(2)}) %collective-permute-start.2) | collective-permute-done | bytes 131104 | tf_op jit(solution)/shard_map/ppermute | solution.py:95
  17.6 0.0 collective-permute-done.1.refs_1_
  17.6 1.9 %copy-done = bf16[1,96,128,128]{3,2,1,0:T(8,128)(2,1)S(1)} copy-done((bf16[1,96,128,128]{3,2,1,0:T(8,128)(2,1)S(1)}, bf16[1,96,128,128]{3,2,1,0:T(8,128)(2,1)}, u32[]{:S(2)}) %copy-start) | copy-done | bytes 3145752
  19.5 0.7 %copy-done.1 = s32[1,2,96]{2,1,0:T(2,128)S(1)} copy-done((s32[1,2,96]{2,1,0:T(2,128)S(1)}, s32[1,2,96]{2,1,0:T(2,128)}, u32[]{:S(2)}) %copy-start.1) | copy-done | bytes 792
  20.2 3.5 %shard_map.55 = (f32[4,128,128]{2,1,0:T(8,128)S(1)}, bf16[4,128,128]{2,1,0:T(8,128)(2,1)S(1)}, bf16[4,128,128]{2,1,0:T(8,128)(2,1)S(1)}, bf16[4,128,128]{2,1,0:T(8,128)(2,1)S(1)}) custom-call(s32[2,96]{1,0:T(2,128)S(1)} %bitcast.16, s32[2]{0:T(128)S(1)} %pad_add_fusion.place_ref, bf16[4,128,128]{2,1,0:T(8,128)(2,1)S(1)} %collective-permute-done.refs_0_, ...), custom_call_target="tpu_custom_call" | custom-call | flops 402653184 | bytes 3145728 | tf_op jit(solution)/shard_map/pallas_call | solution.py:62
  23.8 1.9 %collective-permute-start.4 = (bf16[4,128,128]{2,1,0:T(8,128)(2,1)S(1)}, bf16[4,128,128]{2,1,0:T(8,128)(2,1)S(1)}, u32[]{:S(2)}, u32[]{:S(2)}) collective-permute-start(bf16[4,128,128]{2,1,0:T(8,128)(2,1)S(1)} %get-tuple-element.10), channel_id=1, source_target_pairs={{0,4},{4,0},{8,12},{12,8},{1,5},{5,1},{9,13},{13,9},{2,6},{6,2},{1... | collective-permute-start | bytes 393224 | tf_op jit(solution)/shard_map/ppermute | solution.py:102
  25.7 2.6 %collective-permute-start.5 = (bf16[4,128,128]{2,1,0:T(8,128)(2,1)S(1)}, bf16[4,128,128]{2,1,0:T(8,128)(2,1)S(1)}, u32[]{:S(2)}, u32[]{:S(2)}) collective-permute-start(bf16[4,128,128]{2,1,0:T(8,128)(2,1)S(1)} %get-tuple-element.11), channel_id=1, source_target_pairs={{0,8},{4,12},{8,0},{12,4},{1,9},{5,13},{9,1},{13,5},{2,10},{6,14},... | collective-permute-start | bytes 393224 | tf_op jit(solution)/shard_map/ppermute | solution.py:102
  28.2 0.0 collective-permute-start.6
  28.3 2.9 %collective-permute-done.4 = bf16[4,128,128]{2,1,0:T(8,128)(2,1)S(1)} collective-permute-done((bf16[4,128,128]{2,1,0:T(8,128)(2,1)S(1)}, bf16[4,128,128]{2,1,0:T(8,128)(2,1)S(1)}, u32[]{:S(2)}, u32[]{:S(2)}) %collective-permute-start.4) | collective-permute-done | bytes 131104 | tf_op jit(solution)/shard_map/ppermute | solution.py:102
  31.1 7.4 %collective-permute-done.5 = bf16[4,128,128]{2,1,0:T(8,128)(2,1)S(1)} collective-permute-done((bf16[4,128,128]{2,1,0:T(8,128)(2,1)S(1)}, bf16[4,128,128]{2,1,0:T(8,128)(2,1)S(1)}, u32[]{:S(2)}, u32[]{:S(2)}) %collective-permute-start.5) | collective-permute-done | bytes 131104 | tf_op jit(solution)/shard_map/ppermute | solution.py:102
  38.6 0.0 collective-permute-done.6
  38.6 0.1 convert_add_fusion
  38.6 0.8 %fusion = bf16[1,512,128]{2,1,0:T(8,128)(2,1)} fusion(f32[512]{0:T(512)S(1)} %bitcast.20, f32[1,512,128]{2,1,0:T(8,128)S(1)} %bitcast.17), kind=kLoop, calls=%fused_computation.1 | loop fusion | flops 131072 | bytes 395264 | tf_op jit(solution)/shard_map/convert_element_type | solution.py:105
  (2 shorter events, 0.0 us)
Async XLA Ops:
  2.5 6.5 %collective-permute-start = (bf16[4,128,128]{2,1,0:T(8,128)(2,1)S(1)}, bf16[4,128,128]{2,1,0:T(8,128)(2,1)S(1)}, u32[]{:S(2)}, u32[]{:S(2)}) collective-permute-start(bf16[4,128,128]{2,1,0:T(8,128)(2,1)S(1)} %bitcast.18), channel_id=1, source_target_pairs={{0,16},{16,0},{1,17},{17,1},{2,18},{18,2},{3,19},{19,3},{4,20},{20... | collective-permute-start | bytes 393224 | tf_op jit(solution)/shard_map/ppermute | solution.py:91
  9.0 5.5 %collective-permute-start.3 = (bf16[4,128,128]{2,1,0:T(8,128)(2,1)S(1)}, bf16[4,128,128]{2,1,0:T(8,128)(2,1)S(1)}, u32[]{:S(2)}, u32[]{:S(2)}) collective-permute-start(bf16[4,128,128]{2,1,0:T(8,128)(2,1)S(1)} %collective-permute-done.refs_0_), channel_id=1, source_target_pairs={{0,3},{1,2},{2,1},{3,0},{4,7},{5,6},{6,5},{7,4},{8,11},{9,10},{10,... | collective-permute-start | bytes 393224 | tf_op jit(solution)/shard_map/ppermute | solution.py:95
  9.4 8.3 %collective-permute-start.2 = (bf16[4,128,128]{2,1,0:T(8,128)(2,1)S(1)}, bf16[4,128,128]{2,1,0:T(8,128)(2,1)S(1)}, u32[]{:S(2)}, u32[]{:S(2)}) collective-permute-start(bf16[4,128,128]{2,1,0:T(8,128)(2,1)S(1)} %collective-permute-done.refs_0_), channel_id=1, source_target_pairs={{0,2},{1,3},{2,0},{3,1},{4,6},{5,7},{6,4},{7,5},{8,10},{9,11},{10,... | collective-permute-start | bytes 393224 | tf_op jit(solution)/shard_map/ppermute | solution.py:95
  10.8 6.8 %collective-permute-start.1 = (bf16[4,128,128]{2,1,0:T(8,128)(2,1)S(1)}, bf16[4,128,128]{2,1,0:T(8,128)(2,1)S(1)}, u32[]{:S(2)}, u32[]{:S(2)}) collective-permute-start(bf16[4,128,128]{2,1,0:T(8,128)(2,1)S(1)} %collective-permute-done.refs_0_), channel_id=1, source_target_pairs={{0,1},{1,0},{2,3},{3,2},{4,5},{5,4},{6,7},{7,6},{8,9},{9,8},{10,11... | collective-permute-start | bytes 393224 | tf_op jit(solution)/shard_map/ppermute | solution.py:95
  17.6 1.9 %copy-start = (bf16[1,96,128,128]{3,2,1,0:T(8,128)(2,1)S(1)}, bf16[1,96,128,128]{3,2,1,0:T(8,128)(2,1)}, u32[]{:S(2)}) copy-start(bf16[1,96,128,128]{3,2,1,0:T(8,128)(2,1)} %param.8) | copy-start | bytes 9437188
  19.5 0.7 %copy-start.1 = (s32[1,2,96]{2,1,0:T(2,128)S(1)}, s32[1,2,96]{2,1,0:T(2,128)}, u32[]{:S(2)}) copy-start(s32[1,2,96]{2,1,0:T(2,128)} %param.9) | copy-start | bytes 2308
  23.8 7.4 %collective-permute-start.4 = (bf16[4,128,128]{2,1,0:T(8,128)(2,1)S(1)}, bf16[4,128,128]{2,1,0:T(8,128)(2,1)S(1)}, u32[]{:S(2)}, u32[]{:S(2)}) collective-permute-start(bf16[4,128,128]{2,1,0:T(8,128)(2,1)S(1)} %get-tuple-element.10), channel_id=1, source_target_pairs={{0,4},{4,0},{8,12},{12,8},{1,5},{5,1},{9,13},{13,9},{2,6},{6,2},{1... | collective-permute-start | bytes 393224 | tf_op jit(solution)/shard_map/ppermute | solution.py:102
  25.7 12.9 %collective-permute-start.5 = (bf16[4,128,128]{2,1,0:T(8,128)(2,1)S(1)}, bf16[4,128,128]{2,1,0:T(8,128)(2,1)S(1)}, u32[]{:S(2)}, u32[]{:S(2)}) collective-permute-start(bf16[4,128,128]{2,1,0:T(8,128)(2,1)S(1)} %get-tuple-element.11), channel_id=1, source_target_pairs={{0,8},{4,12},{8,0},{12,4},{1,9},{5,13},{9,1},{13,5},{2,10},{6,14},... | collective-permute-start | bytes 393224 | tf_op jit(solution)/shard_map/ppermute | solution.py:102
  28.2 10.3 %collective-permute-start.6 = (bf16[4,128,128]{2,1,0:T(8,128)(2,1)S(1)}, bf16[4,128,128]{2,1,0:T(8,128)(2,1)S(1)}, u32[]{:S(2)}, u32[]{:S(2)}) collective-permute-start(bf16[4,128,128]{2,1,0:T(8,128)(2,1)S(1)} %get-tuple-element.12), channel_id=1, source_target_pairs={{0,12},{4,8},{8,4},{12,0},{1,13},{5,9},{9,5},{13,1},{2,14},{6,10},... | collective-permute-start | bytes 393224 | tf_op jit(solution)/shard_map/ppermute | solution.py:102
